TPU v7x, 32 devices: a whole 2x2x4 slice. The times are simulated.
32 devices in a mesh: groups: 2 (over y), ha: 4 (over z), ta: 2 (over x), col: 2 (over core).
Axes of the slice: x: 2, y: 2, z: 4, core: 2. Of those that a mesh axis runs over, the one named last changes fastest.
Arguments:
- tokens: bfloat16 [8, 16, 64, 768], P(('groups', 'ta'), 'ha', None, 'col'), parts along dimension 0, may hold values from -6 to 6
- norm1_gain: float32 [768], replicated, may hold values from 0.4 to 1.6
- w_qkv: bfloat16 [3, 768, 768], P(None, None, 'col'), may hold values from -0.21875 to 0.21875
- w_out: bfloat16 [768, 768], P('col'), may hold values from -0.3125 to 0.3125
- norm2_gain: float32 [768], replicated, may hold values from 0.4 to 1.6
- w_up: bfloat16 [768, 3072], P('ha', 'col'), may hold values from -0.21875 to 0.21875
- w_down: bfloat16 [3072, 768], P('col', 'ha'), may hold values from -0.109375 to 0.109375
Outputs:
- block_out: bfloat16 [8, 16, 64, 768], P(('groups', 'ta'), 'ha', None, 'col'), parts along dimension 0
There are 2 independent parts, one for each index of `groups`. A program takes and returns all parts, laid end to end along the dimension named above; an argument that names none is the same for every part. Nothing has to cross between parts.
All inputs are finite; a program needn't handle non-finite values.
Results may differ from a plain program's by a relative error of at most 0.009.
Values may be sent and summed in bfloat16 or wider, within the bound.
A program may use at most 64 MiB of HBM per device.

v0:
```python
import math
import jax
import jax.numpy as jnp
from jax import lax
from jax.sharding import PartitionSpec as P

HD = 64
EPS = 1e-05


def layer_norm(values, gain):
    mean = jnp.mean(values, -1, keepdims=True)
    centred = values - mean
    spread = jnp.mean(centred * centred, -1, keepdims=True)
    return centred * lax.rsqrt(spread + EPS) * gain


def attend(query, keys, values, dim):
    scale = 1.0 / math.sqrt(HD)
    moved_q = jnp.moveaxis(query, dim, -2)
    moved_k = jnp.moveaxis(keys, dim, -2)
    moved_v = jnp.moveaxis(values, dim, -2)
    shape = moved_q.shape
    split = shape[:-1] + (shape[-1] // HD, HD)
    scores = (
        jnp.einsum(
            "...qhd,...khd->...hqk",
            moved_q.reshape(split),
            moved_k.reshape(split),
            preferred_element_type=jnp.float32,
        )
        * scale
    )
    weights = jnp.exp(scores)
    weights = (weights / jnp.sum(weights, -1, keepdims=True)).astype(jnp.bfloat16)
    result = jnp.einsum(
        "...hqk,...khd->...qhd", weights, moved_v.reshape(split), preferred_element_type=jnp.float32
    ).astype(jnp.bfloat16)
    return jnp.moveaxis(result.reshape(shape), -2, dim)


def on_device(tokens, norm1_gain, w_qkv, w_out, norm2_gain, w_up, w_down):
    whole = lax.all_gather(tokens, "col", axis=3, tiled=True)
    frames, rows_h, width, model = whole.shape
    count = frames * rows_h * width
    half = tokens.shape[3]
    wide = whole.astype(jnp.float32).reshape(count, model)
    normed = layer_norm(wide, norm1_gain).astype(jnp.bfloat16)
    stacked = jnp.einsum("rd,sdc->src", normed, w_qkv, preferred_element_type=jnp.float32).astype(
        jnp.bfloat16
    )
    stacked = stacked.reshape(3, frames, rows_h, width, half)
    along_w = attend(stacked[0], stacked[1], stacked[2], 2)
    columns = lax.all_to_all(stacked, "ha", split_axis=3, concat_axis=2, tiled=True)
    along_h_far = attend(columns[0], columns[1], columns[2], 1)
    along_h = lax.all_to_all(along_h_far, "ha", split_axis=1, concat_axis=2, tiled=True)
    lines = lax.all_to_all(stacked, "ta", split_axis=3, concat_axis=1, tiled=True)
    along_t_far = attend(lines[0], lines[1], lines[2], 0)
    along_t = lax.all_to_all(along_t_far, "ta", split_axis=0, concat_axis=2, tiled=True)
    mixed = (
        along_w.astype(jnp.float32) + along_h.astype(jnp.float32) + along_t.astype(jnp.float32)
    ).astype(jnp.bfloat16)
    terms = jnp.dot(mixed.reshape(count, half), w_out, preferred_element_type=jnp.float32)
    offset = lax.axis_index("col") * half
    summed = lax.psum(terms, "col")
    first_full = wide + summed
    second = layer_norm(first_full, norm2_gain).astype(jnp.bfloat16)
    first = lax.dynamic_slice_in_dim(first_full, offset, half, 1)
    upper = jnp.dot(
        second, lax.all_gather(w_up, "ha", axis=0, tiled=True), preferred_element_type=jnp.float32
    )
    hidden = jax.nn.gelu(upper, approximate=False).astype(jnp.bfloat16)
    down_terms = jnp.dot(
        hidden, lax.all_gather(w_down, "ha", axis=1, tiled=True), preferred_element_type=jnp.float32
    )
    down_share = lax.psum_scatter(
        down_terms.astype(jnp.bfloat16), "col", scatter_dimension=1, tiled=True
    ).astype(jnp.float32)
    return (first + down_share).astype(jnp.bfloat16).reshape(frames, rows_h, width, half)


def solution(mesh):
    placed = (
        P(("groups", "ta"), "ha", None, "col"),
        P(),
        P(None, None, "col"),
        P("col", None),
        P(),
        P("ha", "col"),
        P("col", "ha"),
    )
    return jax.shard_map(
        on_device,
        mesh=mesh,
        in_specs=placed,
        out_specs=P(("groups", "ta"), "ha", None, "col"),
        check_vma=False,
    )
```

profile of v0, /device:TPU:0, one launch (start us, length us, event | category | flops | bytes accessed | tf_op | source)
XLA Modules:
  0.0 270.8 jit_solution(178408443112723178)
XLA Ops:
  7.4 2.8 %all_gather.9 = bf16[2,4,64,768]{3,2,1,0:T(8,128)(2,1)S(1)} all-gather(bf16[2,4,64,384]{3,2,1,0:T(8,128)(2,1)} %param.7), channel_id=1, replica_groups=mesh['groups'=2,'ha'=4,'ta'=2,'col'=2] {'col'}, dimensions={3}, use_global_device_ids=true | all-gather | bytes 1179648 | tf_op jit(solution)/shard_map/all_gather | solution.py:43
  15.4 19.9 %all_to_all.48 = bf16[3,2,4,64,384]{4,2,1,0,3:T(4,128)(2,1)} all-to-all(bf16[3,2,4,64,384]{4,2,1,0,3:T(4,128)(2,1)S(1)} %copy.127), channel_id=1, replica_groups=mesh['groups'=2,'ha'=4,'ta'=2,'col'=2] {'ta'}, dimensions={3} | all-to-all | bytes 2359296 | tf_op jit(solution)/shard_map/all_to_all | solution.py:57
  35.3 5.1 %all-to-all-start = ((bf16[3,2,4,64,384]{4,2,1,0,3:T(4,128)(2,1)}), bf16[3,2,4,64,384]{4,2,1,0,3:T(4,128)(2,1)}, u32[]{:S(2)}, u32[]{:S(2)}) async-start(bf16[3,2,4,64,384]{4,2,1,0,3:T(4,128)(2,1)} %copy-done.1), calls=%async_computation | async-start | bytes 2359296 | tf_op jit(solution)/shard_map/all_to_all | solution.py:54
  42.5 2.4 reshape.133
  49.6 2.4 reshape.139
  56.2 3.9 %fusion.23 = f32[4,32,6,4,4]{3,4,2,1,0:T(4,128)} fusion(bf16[4,32,4,6,64]{4,3,1,0,2:T(8,128)(2,1)} %reshape.140, bf16[4,32,4,6,64]{4,3,1,0,2:T(8,128)(2,1)} %reshape.139), kind=kOutput, calls=%fused_computation.46 | convolution fusion | flops 1572864 | bytes 835584 | tf_op jit(solution)/shard_map/...qhd,...khd->...hqk/dot_general | solution.py:26
  68.4 2.4 fusion.21
  74.7 4.4 %all-to-all-start.3 = ((bf16[4,4,32,384]{3,2,1,0:T(8,128)(2,1)}), bf16[4,4,32,384]{3,2,1,0:T(8,128)(2,1)}, u32[]{:S(2)}, u32[]{:S(2)}) async-start(bf16[4,4,32,384]{3,2,1,0:T(8,128)(2,1)} %copy.158), calls=%async_computation.3 | async-start | bytes 786432 | tf_op jit(solution)/shard_map/all_to_all | solution.py:59
  86.4 2.4 reshape.137
  89.6 2.4 reshape.135
  92.1 3.8 %multiply_exponential_fusion = f32[2,16,6,16,16]{3,4,2,1,0:T(8,128)} fusion(bf16[2,16,16,6,64]{4,3,1,2,0:T(8,128)(2,1)} %reshape.137, bf16[2,16,16,6,64]{4,3,1,2,0:T(8,128)(2,1)} %reshape.136), kind=kOutput, calls=%fused_computation.32 | convolution fusion | flops 6340608 | bytes 983040 | tf_op jit(solution)/shard_map/...qhd,...khd->...hqk/dot_general | solution.py:26
  95.9 3.9 %fusion.20 = bf16[2,16,16,6,64]{4,2,3,1,0:T(8,128)(2,1)} fusion(f32[2,16,6,16,16]{3,4,2,1,0:T(8,128)} %multiply_exponential_fusion, bf16[2,16,16,6,64]{4,3,1,2,0:T(8,128)(2,1)} %reshape.135), kind=kOutput, calls=%fused_computation.41 | convolution fusion | flops 6589455 | bytes 983040 | tf_op jit(solution)/shard_map/...hqk,...khd->...qhd/dot_general | solution.py:36
  104.9 5.1 %all-to-all-start.1 = ((bf16[2,16,16,384]{3,2,0,1:T(8,128)(2,1)}), bf16[2,16,16,384]{3,2,0,1:T(8,128)(2,1)}, u32[]{:S(2)}, u32[]{:S(2)}) async-start(bf16[2,16,16,384]{3,2,0,1:T(8,128)(2,1)} %copy.140), calls=%async_computation.1 | async-start | bytes 786432 | tf_op jit(solution)/shard_map/all_to_all | solution.py:56
  110.0 3.3 %multiply_exponential_fusion.1 = f32[2,4,6,64,64]{3,4,2,1,0:T(8,128)} fusion(bf16[2,4,64,6,64]{4,3,2,1,0:T(8,128)(2,1)} %reshape.134, bf16[2,4,64,6,64]{4,3,2,1,0:T(8,128)(2,1)} %reshape.133), kind=kOutput, calls=%fused_computation.34 | convolution fusion | flops 25362432 | bytes 1572864 | tf_op jit(solution)/shard_map/...qhd,...khd->...hqk/dot_general | solution.py:26
  114.8 3.8 %convert_bitcast_fusion = f32[2,4,64,6,64]{2,4,3,1,0:T(8,128)} fusion(f32[2,4,6,64,64]{3,4,2,1,0:T(8,128)} %multiply_exponential_fusion.1, bf16[2,4,64,6,64]{4,3,2,1,0:T(8,128)(2,1)} %reshape.132), kind=kOutput, calls=%fused_computation.28 | convolution fusion | flops 25955392 | bytes 1966080 | tf_op jit(solution)/shard_map/...hqk,...khd->...qhd/dot_general | solution.py:36
  118.6 3.6 %copy.126 = f32[2,4,64,6,64]{2,1,0,4,3:T(4,128)} copy(f32[2,4,64,6,64]{2,4,3,1,0:T(8,128)} %convert_bitcast_fusion) | data formatting | bytes 1572864 | tf_op jit(solution)/shard_map/convert_element_type | solution.py:61
  122.2 3.1 %reshape.126 = f32[512,384]{0,1:T(8,128)} reshape(f32[2,4,64,6,64]{2,1,0,4,3:T(4,128)} %copy.126) | data formatting | bytes 1572864 | tf_op jit(solution)/shard_map/convert_element_type | solution.py:61
  130.0 3.6 %fusion.44 = f32[512,768]{1,0:T(8,128)} fusion(bf16[384,768]{1,0:T(8,128)(2,1)} %param.10, f32[512,384]{0,1:T(8,128)} %copy.160, f32[512,384]{0,1:T(8,128)} %reshape.126, f32[512,384]{0,1:T(8,128)} %copy.143), kind=kOutput, calls=%fused_computation.64 | convolution fusion | flops 302579712 | bytes 4521984 | tf_op jit(solution)/shard_map/dot_general | solution.py:63
  135.1 20.9 %all-reduce.2.cloned.1.call-done = f32[512,768]{1,0:T(8,128)} async-done(((f32[512,768]{1,0:T(8,128)}), f32[512,768]{1,0:T(8,128)}) %all-reduce.2.cloned.1.call-update) | async-done | bytes 1572880 | tf_op jit(solution)/shard_map/psum | solution.py:65
  159.1 28.4 %all-gather.3.cloned.1.call-done = bf16[768,1536]{1,0:T(8,128)(2,1)} async-done(((bf16[192,1536]{1,0:T(8,128)(2,1)}), bf16[768,1536]{1,0:T(8,128)(2,1)}) %all-gather.3.cloned.1.call-update) | async-done | bytes 2359312 | tf_op jit(solution)/shard_map/all_gather | solution.py:70
  187.6 50.3 %all-gather.5.cloned.1.call-done = bf16[1536,768]{0,1:T(8,128)(2,1)} async-done(((bf16[1536,192]{0,1:T(8,128)(2,1)}), bf16[1536,768]{0,1:T(8,128)(2,1)}) %all-gather.5.cloned.1.call-update) | async-done | bytes 2359312 | tf_op jit(solution)/shard_map/all_gather | solution.py:74
  237.8 12.3 %fusion.17 = bf16[512,768]{1,0:T(8,128)(2,1)} fusion(bf16[1536,768]{0,1:T(8,128)(2,1)} %all-gather.5.cloned.1.call-done, bf16[768,1536]{1,0:T(8,128)(2,1)} %all-gather.3.cloned.1.call-done, f32[512,768]{1,0:T(8,128)} %copy-done.2, f32[768]{0:T(1024)S(1)} %copy-done.6, f32[512]{0:T(512)S(1)} %add_rsqrt_fusion.1, f32[512]{0:T(512)S(1)} %broadcast_multiply_fusion.1), kind=kOutput, calls=%fused_computation.37 | convolution fusion | flops 2469003264 | bytes 7085056 | tf_op jit(solution)/shard_map/dot_general | solution.py:73
  250.1 2.4 copy.181
  252.6 7.0 %reduce-scatter.4.cloned.1.call-done = bf16[384,512]{1,0:T(8,128)(2,1)} async-done(((bf16[768,512]{1,0:T(8,128)(2,1)}), bf16[384,512]{1,0:T(8,128)(2,1)}) %reduce-scatter.4.cloned.1.call-update) | async-done | bytes 393232
  (73 shorter events, 56.0 us)
Async XLA Ops:
  7.4 3.8 %copy-start = (bf16[3,768,384]{2,1,0:T(8,128)(2,1)S(1)}, bf16[3,768,384]{2,1,0:T(8,128)(2,1)}, u32[]{:S(2)}) copy-start(bf16[3,768,384]{2,1,0:T(8,128)(2,1)} %param.9) | copy-start | bytes 5308420
  7.4 3.5 %copy-start.5 = (f32[768]{0:T(1024)S(1)}, f32[768]{0:T(1024)}, u32[]{:S(2)}) copy-start(f32[768]{0:T(1024)} %param.8) | copy-start | bytes 9220
  12.4 1.0 copy-start.4
  14.4 1.0 copy-start.1
  35.3 39.4 %all-to-all-start = ((bf16[3,2,4,64,384]{4,2,1,0,3:T(4,128)(2,1)}), bf16[3,2,4,64,384]{4,2,1,0,3:T(4,128)(2,1)}, u32[]{:S(2)}, u32[]{:S(2)}) async-start(bf16[3,2,4,64,384]{4,2,1,0,3:T(4,128)(2,1)} %copy-done.1), calls=%async_computation | async-start | bytes 2359296 | tf_op jit(solution)/shard_map/all_to_all | solution.py:54
  74.7 30.2 %all-to-all-start.3 = ((bf16[4,4,32,384]{3,2,1,0:T(8,128)(2,1)}), bf16[4,4,32,384]{3,2,1,0:T(8,128)(2,1)}, u32[]{:S(2)}, u32[]{:S(2)}) async-start(bf16[4,4,32,384]{3,2,1,0:T(8,128)(2,1)} %copy.158), calls=%async_computation.3 | async-start | bytes 786432 | tf_op jit(solution)/shard_map/all_to_all | solution.py:59
  104.9 22.8 %all-to-all-start.1 = ((bf16[2,16,16,384]{3,2,0,1:T(8,128)(2,1)}), bf16[2,16,16,384]{3,2,0,1:T(8,128)(2,1)}, u32[]{:S(2)}, u32[]{:S(2)}) async-start(bf16[2,16,16,384]{3,2,0,1:T(8,128)(2,1)} %copy.140), calls=%async_computation.1 | async-start | bytes 786432 | tf_op jit(solution)/shard_map/all_to_all | solution.py:56
  110.0 46.1 %all-reduce.2.cloned.1.call-start = ((), (), s32[]{:S(2)}) async-start(), calls=%async_computation.5 | async-start | bytes 3145728 | tf_op jit(solution)/shard_map/psum | solution.py:65
  133.7 53.9 %all-gather.3.cloned.1.call-start = ((), (), s32[]{:S(2)}) async-start(), calls=%async_computation.6 | async-start | bytes 2949120 | tf_op jit(solution)/shard_map/all_gather | solution.py:70
  134.2 103.6 %all-gather.5.cloned.1.call-start = ((), (), s32[]{:S(2)}) async-start(), calls=%async_computation.7 | async-start | bytes 2949120 | tf_op jit(solution)/shard_map/all_gather | solution.py:74
  134.8 103.0 %copy-start.6 = (f32[768]{0:T(1024)S(1)}, f32[768]{0:T(1024)}, u32[]{:S(2)}) copy-start(f32[768]{0:T(1024)} %param.11) | copy-start | bytes 9220
  134.8 124.8 %reduce-scatter.4.cloned.1.call-start = ((), (), s32[]{:S(2)}) async-start(), calls=%async_computation.8 | async-start | bytes 1179648
  157.7 1.2 copy-start.2
  250.1 11.4 %copy-start.3 = (f32[512,768]{1,0:T(8,128)S(1)}, f32[512,768]{1,0:T(8,128)}, u32[]{:S(2)}) copy-start(f32[512,768]{1,0:T(8,128)} %copy-done.2) | copy-start | bytes 4718596
Sparse Core Ops, SparseCore 0:
  133.8 22.2 all-reduce.1
  252.7 6.8 reduce-scatter.3
Sparse Core Ops, SparseCore 1:
  135.8 51.7 all-gather.2
  189.1 48.7 all-gather.4
where the time goes:
time: 272 us; the launch traced here: 271 us
  waiting for transfers between devices  108 us (40%)
  local copies, waits for them, and re-layouts  65.5 us (24%)
  matrix products  38.2 us (14%)
  blocking collectives  22.7 us (8%)
  between operations  15 us (6%)
  starting transfers between devices  14.9 us (5%)
  other arithmetic  6.71 us (2%)
    all_gather x1, waiting for transfers between devices, on_device(): lax.all_gather(w_down, 'ha', axis=1, tiled=True)  50.3 us
    all_gather x1, waiting for transfers between devices, on_device(): lax.all_gather(w_up, 'ha', axis=0, tiled=True)  28.4 us
    psum x1, waiting for transfers between devices, on_device(): summed = lax.psum(terms, 'col')  20.9 us
    all_to_all x1, blocking collectives, on_device(): lax.all_to_all(stacked, 'ta', split_axis=3, concat_axis=1, tiled=True)  19.9 us
    dot_general x1, matrix products, on_device(): jnp.dot(hidden, lax.all_gather(w_down, 'ha', axis=1, tiled=True), preferr...  12.3 us
    dot_general x3, matrix products, attend(): jnp.einsum('...qhd,...khd->...hqk', moved_q.reshape(split), moved_k.resha...  10.9 us
    dot_general x3, matrix products, attend(): jnp.einsum('...hqk,...khd->...qhd', weights, moved_v.reshape(split), pref...  10.2 us
    unnamed x5, waiting for transfers between devices  8.13 us
  transfers between devices with their start and end apart: 7, of which 4 were waited for; matrix products, arithmetic and copies ran while one was open for 29% of the time, Pallas kernels for 0%

commit v1 on v0

--- a/solution.py
+++ b/solution.py
@@ -62,7 +62,7 @@
     ).astype(jnp.bfloat16)
     terms = jnp.dot(mixed.reshape(count, half), w_out, preferred_element_type=jnp.float32)
     offset = lax.axis_index("col") * half
-    summed = lax.psum(terms, "col")
+    summed = jnp.sum(lax.all_gather(terms, "col"), axis=0)
     first_full = wide + summed
     second = layer_norm(first_full, norm2_gain).astype(jnp.bfloat16)
     first = lax.dynamic_slice_in_dim(first_full, offset, half, 1)

time: 272 us -> 282 us (1.037)
  other arithmetic: 6.71 us -> 14.6 us
  waiting for transfers between devices: 108 us -> 115 us
  local copies, waits for them, and re-layouts: 65.5 us -> 62.4 us
    psum x1 -> x0, waiting for transfers between devices: 20.9 us -> none  [on_device(): summed = lax.psum(terms, 'col')]
    all_gather x1, waiting for transfers between devices: 28.4 us -> 43.4 us  [on_device(): lax.all_gather(w_up, 'ha', axis=0, tiled=True)]
    all_gather x0 -> x1, waiting for transfers between devices: none -> 12.3 us  [on_device(): summed = jnp.sum(lax.all_gather(terms, 'col'), axis=0)]
    reduce_sum x0 -> x1, other arithmetic: none -> 3.49 us  [on_device(): summed = jnp.sum(lax.all_gather(terms, 'col'), axis=0)]
    unnamed x16 -> x12, local copies, waits for them, and re-layouts: 7.54 us -> 4.43 us
  transfers between devices with their start and end apart: 7 -> 7, of which waited for: 4 -> 4; matrix products, arithmetic and copies ran while one was open for 29% -> 31% of each run, Pallas kernels for 0% -> 0%
where the time goes in v1:
time: 282 us; the launch traced here: 280 us
  waiting for transfers between devices  115 us (41%)
  local copies, waits for them, and re-layouts  62.4 us (22%)
  matrix products  37.3 us (13%)
  blocking collectives  22.7 us (8%)
  starting transfers between devices  14.9 us (5%)
  other arithmetic  14.6 us (5%)
  between operations  13.3 us (5%)
    all_gather x1, waiting for transfers between devices, on_device(): lax.all_gather(w_down, 'ha', axis=1, tiled=True)  50.9 us
    all_gather x1, waiting for transfers between devices, on_device(): lax.all_gather(w_up, 'ha', axis=0, tiled=True)  43.4 us
    all_to_all x1, blocking collectives, on_device(): lax.all_to_all(stacked, 'ta', split_axis=3, concat_axis=1, tiled=True)  19.9 us
    all_gather x1, waiting for transfers between devices, on_device(): summed = jnp.sum(lax.all_gather(terms, 'col'), axis=0)  12.3 us
    dot_general x1, matrix products, on_device(): jnp.dot(hidden, lax.all_gather(w_down, 'ha', axis=1, tiled=True), preferr...  11.4 us
    dot_general x3, matrix products, attend(): jnp.einsum('...qhd,...khd->...hqk', moved_q.reshape(split), moved_k.resha...  10.9 us
    dot_general x3, matrix products, attend(): jnp.einsum('...hqk,...khd->...qhd', weights, moved_v.reshape(split), pref...  10.2 us
    unnamed x5, waiting for transfers between devices  8.62 us
  transfers between devices with their start and end apart: 7, of which 4 were waited for; matrix products, arithmetic and copies ran while one was open for 31% of the time, Pallas kernels for 0%

profile of v1, /device:TPU:0, one launch (start us, length us, event | category | flops | bytes accessed | tf_op | source)
XLA Modules:
  0.0 280.4 jit_solution(16418462198487933664)
XLA Ops:
  6.5 2.8 all_gather.15
  14.6 19.9 %all_to_all.48 = bf16[3,2,4,64,384]{4,2,1,0,3:T(4,128)(2,1)} all-to-all(bf16[3,2,4,64,384]{4,2,1,0,3:T(4,128)(2,1)S(1)} %copy.127), channel_id=1, replica_groups=mesh['groups'=2,'ha'=4,'ta'=2,'col'=2] {'ta'}, dimensions={3} | all-to-all | bytes 2359296 | tf_op jit(solution)/shard_map/all_to_all | solution.py:57
  34.5 5.1 %all-to-all-start = ((bf16[3,2,4,64,384]{4,2,1,0,3:T(4,128)(2,1)}), bf16[3,2,4,64,384]{4,2,1,0,3:T(4,128)(2,1)}, u32[]{:S(2)}, u32[]{:S(2)}) async-start(bf16[3,2,4,64,384]{4,2,1,0,3:T(4,128)(2,1)} %copy-done.1), calls=%async_computation | async-start | bytes 2359296 | tf_op jit(solution)/shard_map/all_to_all | solution.py:54
  41.7 2.4 reshape.156
  55.3 3.8 %fusion.24 = f32[4,32,6,4,4]{3,4,2,1,0:T(4,128)} fusion(bf16[4,32,4,6,64]{4,3,1,0,2:T(8,128)(2,1)} %reshape.163, bf16[4,32,4,6,64]{4,3,1,0,2:T(8,128)(2,1)} %reshape.162), kind=kOutput, calls=%fused_computation.48 | convolution fusion | flops 1572864 | bytes 835584 | tf_op jit(solution)/shard_map/...qhd,...khd->...hqk/dot_general | solution.py:26
  65.1 2.4 reshape.161
  67.5 2.4 fusion.21
  73.8 4.3 %all-to-all-start.3 = ((bf16[4,4,32,384]{3,2,1,0:T(8,128)(2,1)}), bf16[4,4,32,384]{3,2,1,0:T(8,128)(2,1)}, u32[]{:S(2)}, u32[]{:S(2)}) async-start(bf16[4,4,32,384]{3,2,1,0:T(8,128)(2,1)} %copy.158), calls=%async_computation.3 | async-start | bytes 786432 | tf_op jit(solution)/shard_map/all_to_all | solution.py:59
  85.5 2.4 reshape.160
  91.0 3.8 %multiply_exponential_fusion = f32[2,16,6,16,16]{3,4,2,1,0:T(8,128)} fusion(bf16[2,16,16,6,64]{4,3,1,2,0:T(8,128)(2,1)} %reshape.160, bf16[2,16,16,6,64]{4,3,1,2,0:T(8,128)(2,1)} %reshape.159), kind=kOutput, calls=%fused_computation.33 | convolution fusion | flops 6340608 | bytes 983040 | tf_op jit(solution)/shard_map/...qhd,...khd->...hqk/dot_general | solution.py:26
  94.8 3.9 %fusion.20 = bf16[2,16,16,6,64]{4,2,3,1,0:T(8,128)(2,1)} fusion(f32[2,16,6,16,16]{3,4,2,1,0:T(8,128)} %multiply_exponential_fusion, bf16[2,16,16,6,64]{4,3,1,2,0:T(8,128)(2,1)} %reshape.158), kind=kOutput, calls=%fused_computation.42 | convolution fusion | flops 6589455 | bytes 983040 | tf_op jit(solution)/shard_map/...hqk,...khd->...qhd/dot_general | solution.py:36
  103.8 5.1 %all-to-all-start.1 = ((bf16[2,16,16,384]{3,2,0,1:T(8,128)(2,1)}), bf16[2,16,16,384]{3,2,0,1:T(8,128)(2,1)}, u32[]{:S(2)}, u32[]{:S(2)}) async-start(bf16[2,16,16,384]{3,2,0,1:T(8,128)(2,1)} %copy.140), calls=%async_computation.1 | async-start | bytes 786432 | tf_op jit(solution)/shard_map/all_to_all | solution.py:56
  108.9 3.2 %multiply_exponential_fusion.1 = f32[2,4,6,64,64]{3,4,2,1,0:T(8,128)} fusion(bf16[2,4,64,6,64]{4,3,2,1,0:T(8,128)(2,1)} %reshape.157, bf16[2,4,64,6,64]{4,3,2,1,0:T(8,128)(2,1)} %reshape.156), kind=kOutput, calls=%fused_computation.35 | convolution fusion | flops 25362432 | bytes 1572864 | tf_op jit(solution)/shard_map/...qhd,...khd->...hqk/dot_general | solution.py:26
  113.7 3.8 %convert_bitcast_fusion = f32[2,4,64,6,64]{2,4,3,1,0:T(8,128)} fusion(f32[2,4,6,64,64]{3,4,2,1,0:T(8,128)} %multiply_exponential_fusion.1, bf16[2,4,64,6,64]{4,3,2,1,0:T(8,128)(2,1)} %reshape.155), kind=kOutput, calls=%fused_computation.29 | convolution fusion | flops 25955392 | bytes 1966080 | tf_op jit(solution)/shard_map/...hqk,...khd->...qhd/dot_general | solution.py:36
  117.6 3.6 %copy.126 = f32[2,4,64,6,64]{2,1,0,4,3:T(4,128)} copy(f32[2,4,64,6,64]{2,4,3,1,0:T(8,128)} %convert_bitcast_fusion) | data formatting | bytes 1572864 | tf_op jit(solution)/shard_map/convert_element_type | solution.py:61
  121.1 3.1 %reshape.148 = f32[512,384]{0,1:T(8,128)} reshape(f32[2,4,64,6,64]{2,1,0,4,3:T(4,128)} %copy.126) | data formatting | bytes 1572864 | tf_op jit(solution)/shard_map/convert_element_type | solution.py:61
  128.9 3.7 %fusion.45 = f32[512,768]{1,0:T(8,128)} fusion(bf16[384,768]{1,0:T(8,128)(2,1)} %param.10, f32[512,384]{0,1:T(8,128)} %copy.160, f32[512,384]{0,1:T(8,128)} %reshape.148, f32[512,384]{0,1:T(8,128)} %copy.143), kind=kOutput, calls=%fused_computation.66 | convolution fusion | flops 302579712 | bytes 4521984 | tf_op jit(solution)/shard_map/dot_general | solution.py:63
  134.4 12.3 %all-gather.9.cloned.1.call-done = f32[1024,768]{1,0:T(8,128)} async-done(((f32[512,768]{1,0:T(8,128)}), f32[1024,768]{1,0:T(8,128)}) %all-gather.9.cloned.1.call-update) | async-done | bytes 3145744 | tf_op jit(solution)/shard_map/all_gather | solution.py:65
  146.7 3.5 %reduce_sum.79 = f32[512,768]{1,0:T(8,128)} reduce(f32[2,512,768]{2,1,0:T(8,128)} %bitcast.103, f32[]{:T(128)} %constant.37.clone.1), dimensions={0}, to_apply=%region_5.0 | reduce | flops 393216 | bytes 4718596 | tf_op jit(solution)/shard_map/reduce_sum | solution.py:65
  153.8 2.8 bitcast_add_fusion
  156.6 43.4 %all-gather.5.cloned.1.call-done = bf16[768,1536]{1,0:T(8,128)(2,1)} async-done(((bf16[192,1536]{1,0:T(8,128)(2,1)}), bf16[768,1536]{1,0:T(8,128)(2,1)}) %all-gather.5.cloned.1.call-update) | async-done | bytes 2359312 | tf_op jit(solution)/shard_map/all_gather | solution.py:70
  200.0 50.9 %all-gather.7.cloned.1.call-done = bf16[1536,768]{0,1:T(8,128)(2,1)} async-done(((bf16[1536,192]{0,1:T(8,128)(2,1)}), bf16[1536,768]{0,1:T(8,128)(2,1)}) %all-gather.7.cloned.1.call-update) | async-done | bytes 2359312 | tf_op jit(solution)/shard_map/all_gather | solution.py:74
  250.9 11.4 %fusion.17 = bf16[512,768]{1,0:T(8,128)(2,1)S(1)} fusion(bf16[1536,768]{0,1:T(8,128)(2,1)} %all-gather.7.cloned.1.call-done, bf16[768,1536]{1,0:T(8,128)(2,1)} %all-gather.5.cloned.1.call-done, f32[512,768]{1,0:T(8,128)} %bitcast_add_fusion, f32[768]{0:T(1024)S(1)} %copy-done.4, f32[512]{0:T(512)S(1)} %rsqrt.25, f32[512]{0:T(512)S(1)} %div.50), kind=kOutput, calls=%fused_computation.38 | convolution fusion | flops 2469003264 | bytes 7085056 | tf_op jit(solution)/shard_map/dot_general | solution.py:73
  263.5 7.2 %reduce-scatter.4.cloned.1.call-done = bf16[384,512]{1,0:T(8,128)(2,1)} async-done(((bf16[768,512]{1,0:T(8,128)(2,1)}), bf16[384,512]{1,0:T(8,128)(2,1)}) %reduce-scatter.4.cloned.1.call-update) | async-done | bytes 393232
  (73 shorter events, 59.7 us)
Async XLA Ops:
  6.5 3.8 %copy-start = (bf16[3,768,384]{2,1,0:T(8,128)(2,1)S(1)}, bf16[3,768,384]{2,1,0:T(8,128)(2,1)}, u32[]{:S(2)}) copy-start(bf16[3,768,384]{2,1,0:T(8,128)(2,1)} %param.9) | copy-start | bytes 5308420
  6.5 3.5 %copy-start.3 = (f32[768]{0:T(1024)S(1)}, f32[768]{0:T(1024)}, u32[]{:S(2)}) copy-start(f32[768]{0:T(1024)} %param.8) | copy-start | bytes 9220
  11.6 1.0 copy-start.2
  13.5 1.0 copy-start.1
  34.5 39.3 %all-to-all-start = ((bf16[3,2,4,64,384]{4,2,1,0,3:T(4,128)(2,1)}), bf16[3,2,4,64,384]{4,2,1,0,3:T(4,128)(2,1)}, u32[]{:S(2)}, u32[]{:S(2)}) async-start(bf16[3,2,4,64,384]{4,2,1,0,3:T(4,128)(2,1)} %copy-done.1), calls=%async_computation | async-start | bytes 2359296 | tf_op jit(solution)/shard_map/all_to_all | solution.py:54
  73.8 30.1 %all-to-all-start.3 = ((bf16[4,4,32,384]{3,2,1,0:T(8,128)(2,1)}), bf16[4,4,32,384]{3,2,1,0:T(8,128)(2,1)}, u32[]{:S(2)}, u32[]{:S(2)}) async-start(bf16[4,4,32,384]{3,2,1,0:T(8,128)(2,1)} %copy.158), calls=%async_computation.3 | async-start | bytes 786432 | tf_op jit(solution)/shard_map/all_to_all | solution.py:59
  103.8 22.7 %all-to-all-start.1 = ((bf16[2,16,16,384]{3,2,0,1:T(8,128)(2,1)}), bf16[2,16,16,384]{3,2,0,1:T(8,128)(2,1)}, u32[]{:S(2)}, u32[]{:S(2)}) async-start(bf16[2,16,16,384]{3,2,0,1:T(8,128)(2,1)} %copy.140), calls=%async_computation.1 | async-start | bytes 786432 | tf_op jit(solution)/shard_map/all_to_all | solution.py:56
  108.9 37.8 %all-gather.9.cloned.1.call-start = ((), (), s32[]{:S(2)}) async-start(), calls=%async_computation.7 | async-start | bytes 4718592 | tf_op jit(solution)/shard_map/all_gather | solution.py:65
  132.6 67.3 %all-gather.5.cloned.1.call-start = ((), (), s32[]{:S(2)}) async-start(), calls=%async_computation.5 | async-start | bytes 2949120 | tf_op jit(solution)/shard_map/all_gather | solution.py:70
  133.4 117.5 %all-gather.7.cloned.1.call-start = ((), (), s32[]{:S(2)}) async-start(), calls=%async_computation.6 | async-start | bytes 2949120 | tf_op jit(solution)/shard_map/all_gather | solution.py:74
  134.1 136.6 %reduce-scatter.4.cloned.1.call-start = ((), (), s32[]{:S(2)}) async-start(), calls=%async_computation.8 | async-start | bytes 1179648
  153.7 97.2 %copy-start.4 = (f32[768]{0:T(1024)S(1)}, f32[768]{0:T(1024)}, u32[]{:S(2)}) copy-start(f32[768]{0:T(1024)} %param.11) | copy-start | bytes 9220
Sparse Core Ops, SparseCore 0:
  132.8 13.9 all-gather.8
  148.3 51.6 all-gather.4
  201.6 49.2 all-gather.6
  263.6 7.0 reduce-scatter.3
